TPU v7x, 32 devices: a whole 2x2x4 slice. The times are simulated.
32 devices in a mesh: site: 16 (over z, x, core), col: 2 (over y).
Axes of the slice: x: 2, y: 2, z: 4, core: 2. Of those that a mesh axis runs over, the one named last changes fastest.
Arguments:
- panel: bfloat16 [2, 32768, 1024], P(None, 'site', 'col'), may hold values from -0.03125 to 0.03125
- xs: int32 [32768], P(('site', 'col')), may hold values from 0 to 255, as said below
- ys: int32 [32768], P(('site', 'col')), may hold values from 0 to 127
Outputs:
- marker: float32 [32768], P(('site', 'col'))
Inputs may be any that keep to these rules, and one draw needn't show every extreme that they name: The pairs (xs, ys) list every cell of a 256 by 128 lattice exactly once.
All inputs are finite; a program needn't handle non-finite values.
Results may differ from a plain program's by a relative error of at most 0.008.
Values may be sent and summed in bfloat16 or wider, within the bound.
A program may use at most 128 MiB of HBM per device.

v0:
```python
import math

import jax
import jax.numpy as jnp
from jax import lax
from jax.sharding import PartitionSpec as P

LX = 256


def commute(owned, arrived, panel_width):
    gx_real = owned[:, :panel_width]
    gx_imag = owned[:, panel_width : 2 * panel_width]
    gy_real = owned[:, 2 * panel_width : 3 * panel_width]
    gy_imag = owned[:, 3 * panel_width :]
    px_real = arrived[:, :panel_width]
    px_imag = arrived[:, panel_width : 2 * panel_width]
    py_real = arrived[:, 2 * panel_width : 3 * panel_width]
    py_imag = arrived[:, 3 * panel_width :]
    factor = jnp.concatenate([gx_real, gx_imag, gy_real, gy_imag], axis=1)
    blocks = jnp.concatenate(
        [
            jnp.concatenate([py_real, py_imag], axis=1),
            jnp.concatenate([-py_imag, py_real], axis=1),
            jnp.concatenate([-px_real, -px_imag], axis=1),
            jnp.concatenate([px_imag, -px_real], axis=1),
        ],
        axis=0,
    )
    return jnp.dot(factor, blocks, preferred_element_type=jnp.float32)


def shards(panel, xs, ys):
    slab = lax.all_to_all(panel, "col", split_axis=1, concat_axis=2, tiled=True)
    row_count = slab.shape[1]
    panel_width = slab.shape[2]
    devices = lax.axis_size("site") * lax.axis_size("col")
    lat_y = row_count * devices // LX
    centre_x = xs.astype(jnp.float32) - (LX - 1) / 2.0
    centre_y = ys.astype(jnp.float32) - (lat_y - 1) / 2.0
    slab_real = slab[0]
    slab_imag = slab[1]
    xw_real = (centre_x[:, None] * slab_real).astype(jnp.bfloat16)
    xw_imag = (centre_x[:, None] * slab_imag).astype(jnp.bfloat16)
    yw_real = (centre_y[:, None] * slab_real).astype(jnp.bfloat16)
    yw_imag = (centre_y[:, None] * slab_imag).astype(jnp.bfloat16)
    stacked = jnp.concatenate([slab_real, slab_imag], axis=0)
    weighted = jnp.concatenate(
        [
            jnp.concatenate([xw_real, xw_imag, yw_real, yw_imag], axis=1),
            jnp.concatenate([xw_imag, -xw_real, yw_imag, -yw_real], axis=1),
        ],
        axis=0,
    )
    own_rows = panel_width // devices
    total_sum = lax.psum(
        lax.dot_general(
            stacked, weighted, (((0,), (0,)), ((), ())), preferred_element_type=jnp.float32
        ),
        ("site", "col"),
    )
    summed = total_sum.astype(jnp.bfloat16)
    owned = lax.dynamic_slice_in_dim(
        summed, lax.axis_index(("site", "col")) * own_rows, own_rows, 0
    )
    commutator = commute(owned, summed, panel_width)
    rounded = commutator.astype(jnp.bfloat16)
    arrived = lax.all_gather(rounded, ("site", "col"), axis=0, tiled=True)
    comm_real = arrived[:, :panel_width]
    comm_imag = arrived[:, panel_width:]
    factor = jnp.concatenate([slab_real, slab_imag], axis=1)
    blocks = jnp.concatenate(
        [
            jnp.concatenate([comm_real, comm_imag], axis=1),
            jnp.concatenate([-comm_imag, comm_real], axis=1),
        ],
        axis=0,
    )
    projected = jnp.dot(factor, blocks, preferred_element_type=jnp.float32)
    proj_real = projected[:, :panel_width]
    proj_imag = projected[:, panel_width:]
    return (
        2.0
        * math.pi
        * jnp.sum(
            proj_imag * slab_real.astype(jnp.float32) - proj_real * slab_imag.astype(jnp.float32),
            axis=1,
        )
    )


def solution(mesh):
    placed = (P(None, "site", "col"), P(("site", "col")), P(("site", "col")))
    return jax.shard_map(
        shards, mesh=mesh, in_specs=placed, out_specs=P(("site", "col")), check_vma=False
    )
```

profile of v0, /device:TPU:0, one launch (start us, length us, event | category | flops | bytes accessed | tf_op | source)
XLA Modules:
  0.0 619.7 jit_solution(10455760163166550563)
XLA Ops:
  6.5 10.1 %copy.5 = bf16[2,2048,512]{2,0,1:T(2,128)(2,1)} copy(bf16[2,2048,512]{2,1,0:T(8,128)(2,1)} %param.3) | data formatting | bytes 8388608 | tf_op args[0]
  16.7 0.0 copy-start.3
  16.7 0.0 copy-start.4
  16.7 5.7 all-to-all-start
  22.4 0.0 all-gather.2.cloned.1.call-start
  22.5 0.0 copy-done.3
  22.5 0.0 copy-done.4
  22.5 48.8 %all-to-all-done = bf16[2,2048,512]{2,0,1:T(2,128)(2,1)} async-done(((bf16[2,2048,512]{2,0,1:T(2,128)(2,1)}), bf16[2,2048,512]{2,0,1:T(2,128)(2,1)}, u32[]{:S(2)}, u32[]{:S(2)}) %all-to-all-start) | async-done | bytes 4194336 | tf_op jit(solution)/shard_map/all_to_all | solution.py:34
  71.3 6.5 %copy.10 = bf16[2,2,1024,512]{3,1,2,0:T(2,128)(2,1)S(1)} copy(bf16[2,2,1024,512]{3,0,2,1:T(2,128)(2,1)} %bitcast) | data formatting | bytes 8388608 | tf_op jit(solution)/shard_map/all_to_all | solution.py:34
  77.8 3.0 fusion.60
  80.8 0.6 copy.7
  81.3 0.0 copy-start
  81.3 0.6 copy.8
  81.9 2.6 fusion.56
  84.5 0.6 fusion.40
  85.2 0.0 copy-done
  85.2 140.4 %fusion = f32[1024,4096]{1,0:T(8,128)} fusion(bf16[1024,1024]{1,0:T(8,128)(2,1)} %get-tuple-element.20, bf16[1024,1024]{1,0:T(8,128)(2,1)S(1)} %get-tuple-element.19, bf16[1024,1024]{1,0:T(8,128)(2,1)S(1)} %get-tuple-element.5, bf16[1024,1024]{1,0:T(8,128)(2,1)S(1)} %get-tuple-element.18, bf16[1024,1024]{1,0:T(8,128)(2,1)} %get-tuple-element.21, ...), kind=kOutput, calls=%fused_computation | convolution fusion | flops 17322475520 | bytes 33554432 | tf_op jit(solution)/shard_map/dot_general | solution.py:57
  225.6 274.8 %all-reduce.1 = bf16[1024,4096]{1,0:T(8,128)(2,1)} all-reduce(f32[1024,4096]{1,0:T(8,128)} %fusion), channel_id=1, replica_groups=mesh['site'=16,'col'=2] {'site','col'}, use_global_device_ids=true, to_apply=%region_0.0 | all-reduce | flops 4194304 | bytes 25165824 | tf_op jit(solution)/shard_map/psum | solution.py:56
  500.4 6.1 slice_negate_fusion.2
  506.5 0.0 slice-start
  506.5 2.2 slice-done
  508.7 17.7 %fusion.48 = bf16[32,2048]{1,0:T(8,128)(2,1)} fusion(bf16[1024,1024]{1,0:T(8,128)(2,1)} %get-tuple-element.11, bf16[1024,1024]{1,0:T(8,128)(2,1)} %get-tuple-element.10, bf16[1024,1024]{1,0:T(8,128)(2,1)} %get-tuple-element.13, bf16[1024,1024]{1,0:T(8,128)(2,1)} %get-tuple-element.12, bf16[1024,1024]{1,0:T(8,128)(2,1)S(1)} %get-tuple-element.9, ...), kind=kOutput, calls=%fused_computation.55 | convolution fusion | flops 654376960 | bytes 15073284 | tf_op jit(solution)/shard_map/dot_general | solution.py:30
  526.4 0.0 all-gather.2.cloned.1.call-update
  526.4 60.1 %all-gather.2.cloned.1.call-done = bf16[1024,2048]{1,0:T(8,128)(2,1)} async-done(((bf16[32,2048]{1,0:T(8,128)(2,1)}), bf16[1024,2048]{1,0:T(8,128)(2,1)}) %all-gather.2.cloned.1.call-update) | async-done | bytes 4194320 | tf_op jit(solution)/shard_map/all_gather | solution.py:68
  586.5 0.0 copy-start.1
  586.5 0.0 copy-start.2
  586.5 4.0 slice_negate_fusion
  590.5 0.0 copy-done.1
  590.5 0.8 copy-done.2
  591.4 16.0 %fusion.30 = f32[1024,2048]{1,0:T(8,128)} fusion(bf16[1024,1024]{1,0:T(8,128)(2,1)} %get-tuple-element.15, bf16[1024,1024]{1,0:T(8,128)(2,1)S(1)} %get-tuple-element.14, bf16[1024,2048]{1,0:T(8,128)(2,1)S(1)} %copy-done.2, bf16[1024,1024]{1,0:T(8,128)(2,1)S(1)} %bitcast.12, bf16[1024,1024]{1,0:T(8,128)(2,1)S(1)} %bitcast.16), kind=kOutput, calls=%fused_computation.30 | convolution fusion | flops 8623489024 | bytes 20971520 | tf_op jit(solution)/shard_map/dot_general | solution.py:79
  607.4 4.3 fusion.39
  611.7 0.6 broadcast_multiply_fusion
  (1 shorter events, 0.0 us)
Async XLA Ops:
  16.7 5.8 copy-start.3
  16.7 5.8 copy-start.4
  16.7 54.6 %all-to-all-start = ((bf16[2,2048,512]{2,0,1:T(2,128)(2,1)}), bf16[2,2048,512]{2,0,1:T(2,128)(2,1)}, u32[]{:S(2)}, u32[]{:S(2)}) async-start(bf16[2,2048,512]{2,0,1:T(2,128)(2,1)} %copy.5), calls=%async_computation | async-start | bytes 8388608 | tf_op jit(solution)/shard_map/all_to_all | solution.py:34
  22.4 564.1 %all-gather.2.cloned.1.call-start = ((), (), s32[]{:S(2)}) async-start(), calls=%async_computation.1 | async-start | bytes 4325376 | tf_op jit(solution)/shard_map/all_gather | solution.py:68
  81.3 3.9 copy-start
  506.5 2.2 slice-start
  586.5 4.0 copy-start.1
  586.5 4.8 copy-start.2
Sparse Core Ops, SparseCore 0:
  526.5 59.9 all-gather.1
where the time goes:
time: 627 us; the launch traced here: 620 us
  blocking collectives  275 us (44%)
  matrix products  174 us (28%)
  waiting for transfers between devices  109 us (17%)
  local copies, waits for them, and re-layouts  23.7 us (4%)
  other arithmetic  18.3 us (3%)
  between operations  14 us (2%)
    psum x1, blocking collectives, shards(): lax.psum(lax.dot_general(stacked, weighted, (((0,), (0,)), ((), ())), pre...  275 us
    dot_general x1, matrix products, shards(): lax.dot_general(stacked, weighted, (((0,), (0,)), ((), ())), preferred_el...  140 us
    all_gather x1, waiting for transfers between devices, shards(): arrived = lax.all_gather(rounded, ('site', 'col'), axis=0, tiled=True)  60.1 us
    all_to_all x1, waiting for transfers between devices, shards(): slab = lax.all_to_all(panel, 'col', split_axis=1, concat_axis=2, tiled=True)  48.8 us
    dot_general x1, matrix products, commute(): return jnp.dot(factor, blocks, preferred_element_type=jnp.float32)  17.7 us
    dot_general x1, matrix products, shards(): projected = jnp.dot(factor, blocks, preferred_element_type=jnp.float32)  16 us
  transfers between devices with their start and end apart: 2, of which 2 were waited for; matrix products, arithmetic and copies ran while one was open for 0% of the time, Pallas kernels for 0%

commit v1 on v0

v1 whole, which is shorter than its diff:
```python
import functools
import math

import jax
import jax.numpy as jnp
from jax import lax
from jax.experimental import pallas as pl
from jax.experimental.pallas import tpu as pltpu
from jax.sharding import PartitionSpec as P

LX = 256
MESH = pl.DeviceIdType.MESH
TN = (((0,), (0,)), ((), ()))


def kernel(groups, panel_ref, cx_ref, cy_ref, out_ref, slab, acc, stage0, recv0, stage1, recv1,
           stage2, recv2, stage3, recv3, full, turned,
           local_sem, swap_send, swap_recv, pair_send, pair_recv, group_send, group_recv,
           gather_send, gather_recv, spread_send, spread_recv):
    rows, width = slab.shape[1], slab.shape[2]
    half = width // 2
    site, col = lax.axis_index("site"), lax.axis_index("col")
    core = site % 2
    pair = (site // 2) % 2
    group = site // 4
    other_core = (site + 1 - 2 * core, col)
    other_pair = (site + 2 - 4 * pair, col)
    other_col = (site, 1 - col)

    def peer(step):
        return (((group + step) % groups) * 4 + pair * 2 + core, col)

    barrier = pltpu.get_barrier_semaphore()
    for target in [other_core, other_pair, other_col] + [peer(d) for d in range(1, groups)]:
        pl.semaphore_signal(barrier, inc=1, device_id=target, device_id_type=MESH)
    pl.semaphore_wait(barrier, 3 + groups - 1)

    def send(src, dst, send_sem, recv_sem, target):
        copy = pltpu.make_async_remote_copy(
            src_ref=src, dst_ref=dst, send_sem=send_sem, recv_sem=recv_sem,
            device_id=target, device_id_type=MESH)
        copy.start()
        return copy

    pieces = 4
    tall = rows // pieces
    my_cols = pl.ds(pl.multiple_of(col * half, half), half)
    swaps, locals_ = [], []
    for k in range(pieces):
        there = pl.ds(pl.multiple_of((1 - col) * rows + k * tall, tall), tall)
        swaps.append(send(panel_ref.at[:, there, :], slab.at[:, pl.ds(k * tall, tall), my_cols],
                          swap_send.at[k], swap_recv.at[k], other_col))
    for k in range(pieces):
        here = pl.ds(pl.multiple_of(col * rows + k * tall, tall), tall)
        copy = pltpu.make_async_copy(
            panel_ref.at[:, here, :], slab.at[:, pl.ds(k * tall, tall), my_cols], local_sem.at[k])
        copy.start()
        locals_.append(copy)

    block = 256

    def gram(k, h):
        piece = pl.ds(k * tall, tall)
        weight = (cx_ref if h == 0 else cy_ref)[piece, :]

        @pl.loop(0, width // block)
        def _(j):
            at = pl.ds(pl.multiple_of(j * block, block), block)
            real = slab[0, piece, at].astype(jnp.float32)
            imag = slab[1, piece, at].astype(jnp.float32)
            first = (weight * (real + imag)).astype(jnp.bfloat16)
            second = (weight * (imag - real)).astype(jnp.bfloat16)
            part = lax.dot_general(first, slab[0, piece, :], TN, preferred_element_type=jnp.float32)
            part += lax.dot_general(second, slab[1, piece, :], TN, preferred_element_type=jnp.float32)
            if k == 0:
                acc[h, at, :] = part
            else:
                acc[h, at, :] += part

    step_rows = 64
    own = pl.ds(pl.multiple_of(core * half, half), half)
    away = pl.ds(pl.multiple_of((1 - core) * half, half), half)

    def aligned(start, size):
        return pl.ds(pl.multiple_of(start, 16), size)

    def begin0(h):
        @pl.loop(0, width // step_rows)
        def _(i):
            at = aligned(i * step_rows, step_rows)
            stage0[h, at, :] = acc[h, at, away].astype(jnp.bfloat16)
        return send(stage0.at[h], recv0.at[h], pair_send.at[0, h], pair_recv.at[0, h], other_core)

    halves = width // 2
    quarter = width // 4
    bits = [(col, pair), (pair, col)]
    targets = [(other_col, other_pair), (other_pair, other_col)]
    base1 = [bits[h][0] * halves for h in range(2)]
    base2 = [base1[h] + bits[h][1] * quarter for h in range(2)]
    chunk = quarter // groups
    base3 = [base2[h] + group * chunk for h in range(2)]

    def begin1(h):
        gone = (1 - bits[h][0]) * halves

        @pl.loop(0, halves // step_rows)
        def _(i):
            at = aligned(gone + i * step_rows, step_rows)
            stage1[h, aligned(i * step_rows, step_rows), :] = (
                acc[h, at, own] + recv0[h, at, :].astype(jnp.float32)).astype(jnp.bfloat16)
        copy = send(stage1.at[h], recv1.at[h], pair_send.at[1, h], pair_recv.at[1, h], targets[h][0])

        @pl.loop(0, halves // step_rows)
        def _(i):
            at = aligned(base1[h] + i * step_rows, step_rows)
            acc[h, at, own] += recv0[h, at, :].astype(jnp.float32)
        return copy

    def begin2(h):
        gone = (1 - bits[h][1]) * quarter
        kept = bits[h][1] * quarter

        @pl.loop(0, quarter // step_rows)
        def _(i):
            inner = aligned(gone + i * step_rows, step_rows)
            at = aligned(base1[h] + gone + i * step_rows, step_rows)
            stage2[h, aligned(i * step_rows, step_rows), :] = (
                acc[h, at, own] + recv1[h, inner, :].astype(jnp.float32)).astype(jnp.bfloat16)
        copy = send(stage2.at[h], recv2.at[h], pair_send.at[2, h], pair_recv.at[2, h], targets[h][1])

        @pl.loop(0, quarter // step_rows)
        def _(i):
            inner = aligned(kept + i * step_rows, step_rows)
            at = aligned(base2[h] + i * step_rows, step_rows)
            acc[h, at, own] += recv1[h, inner, :].astype(jnp.float32)
        return copy

    def begin3(h):
        @pl.loop(0, quarter // step_rows)
        def _(i):
            inner = aligned(i * step_rows, step_rows)
            at = aligned(base2[h] + i * step_rows, step_rows)
            total = acc[h, at, own] + recv2[h, inner, :].astype(jnp.float32)
            acc[h, at, own] = total
            stage3[h, inner, :] = total.astype(jnp.bfloat16)
        copies = []
        for d in range(1, groups):
            to = (group + d) % groups
            copies.append(send(stage3.at[h, aligned(to * chunk, chunk), :], recv3.at[h, d - 1],
                               group_send.at[h, d - 1], group_recv.at[h, d - 1], peer(d)))
        return copies

    def spread(h, rows_at, cols_at, which, target):
        place = full.at[h, rows_at, cols_at]
        return send(place, place, spread_send.at[which, h], spread_recv.at[which, h], target)

    def begin4(h):
        at = aligned(base3[h], chunk)
        total = acc[h, at, own]
        for d in range(1, groups):
            total += recv3[h, d - 1].astype(jnp.float32)
        full[h, at, own] = total.astype(jnp.bfloat16)
        place = full.at[h, at, own]
        return [send(place, place, gather_send.at[h, d - 1], gather_recv.at[h, d - 1], peer(d))
                for d in range(1, groups)]

    def begin5(h):
        return spread(h, aligned(base2[h], quarter), own, 0, targets[h][1])

    def begin6(h):
        return spread(h, aligned(base1[h], halves), own, 1, targets[h][0])

    def begin7(h):
        return spread(h, pl.ds(0, width), own, 2, other_core)

    for k in range(pieces):
        locals_[k].wait()
        swaps[k].wait()
        if k < pieces - 1:
            gram(k, 0)
            gram(k, 1)
    flight = [None, None]
    for h in range(2):
        gram(pieces - 1, h)
        flight[h] = [begin0(h)]
    for begin in (begin1, begin2, begin3, begin4, begin5, begin6, begin7):
        for h in range(2):
            for copy in flight[h]:
                copy.wait()
            started = begin(h)
            flight[h] = started if isinstance(started, list) else [started]
    for h in range(2):
        for copy in flight[h]:
            copy.wait()

    deep = 256

    @pl.loop(0, width // block)
    def _(c):
        at = pl.ds(pl.multiple_of(c * block, block), block)
        for h in range(2):
            turned[h] = full[h, at, :].T

        @pl.loop(0, rows // deep)
        def _(r):
            here = pl.ds(pl.multiple_of(r * deep, deep), deep)
            real, imag = slab[0, here, :], slab[1, here, :]
            dot = functools.partial(jnp.dot, preferred_element_type=jnp.float32)
            ps, qs = [], []
            for h in range(2):
                straight = full[h, :, at]
                ps.append(dot(real, turned[h]) + dot(imag, straight))
                qs.append(dot(imag, turned[h]) - dot(real, straight))
            term = 2.0 * math.pi * jnp.sum(qs[0] * ps[1] - ps[0] * qs[1], axis=1, keepdims=True)

            @pl.when(c == 0)
            def _():
                out_ref[here, :] = term

            @pl.when(c > 0)
            def _():
                out_ref[here, :] += term


def shards(panel, xs, ys):
    rows = panel.shape[1] // lax.axis_size("col")
    width = panel.shape[2] * lax.axis_size("col")
    devices = lax.axis_size("site") * lax.axis_size("col")
    groups = lax.axis_size("site") // 4
    lat_y = rows * devices // LX
    centre_x = xs.astype(jnp.float32) - (LX - 1) / 2.0
    centre_y = ys.astype(jnp.float32) - (lat_y - 1) / 2.0
    half, quarter = width // 2, width // 4
    dma = pltpu.SemaphoreType.DMA
    vmem = pl.BlockSpec(memory_space=pltpu.VMEM)
    out = pl.pallas_call(
        functools.partial(kernel, groups),
        out_shape=jax.ShapeDtypeStruct((rows, 1), jnp.float32),
        in_specs=[pl.BlockSpec(memory_space=pl.ANY), vmem, vmem],
        out_specs=vmem,
        scratch_shapes=[
            pltpu.VMEM((2, rows, width), jnp.bfloat16),
            pltpu.VMEM((2, width, width), jnp.float32),
            pltpu.VMEM((2, width, half), jnp.bfloat16),
            pltpu.VMEM((2, width, half), jnp.bfloat16),
            pltpu.VMEM((2, half, half), jnp.bfloat16),
            pltpu.VMEM((2, half, half), jnp.bfloat16),
            pltpu.VMEM((2, quarter, half), jnp.bfloat16),
            pltpu.VMEM((2, quarter, half), jnp.bfloat16),
            pltpu.VMEM((2, quarter, half), jnp.bfloat16),
            pltpu.VMEM((2, groups - 1, quarter // groups, half), jnp.bfloat16),
            pltpu.VMEM((2, width, width), jnp.bfloat16),
            pltpu.VMEM((2, width, 256), jnp.bfloat16),
            dma((4,)),
            dma((4,)),
            dma((4,)),
            dma((3, 2)),
            dma((3, 2)),
            dma((2, groups - 1)),
            dma((2, groups - 1)),
            dma((2, groups - 1)),
            dma((2, groups - 1)),
            dma((3, 2)),
            dma((3, 2)),
        ],
        compiler_params=pltpu.CompilerParams(
            collective_id=0, has_side_effects=True, vmem_limit_bytes=50 * 1024 * 1024),
    )(panel, centre_x[:, None], centre_y[:, None])
    return out[:, 0]


def solution(mesh):
    placed = (P(None, "site", "col"), P(("site", "col")), P(("site", "col")))
    return jax.shard_map(
        shards, mesh=mesh, in_specs=placed, out_specs=P(("site", "col")), check_vma=False
    )
```

time: 627 us -> 149 us (0.24)
  blocking collectives: 275 us -> 0 us
  matrix products: 174 us -> 0 us
  Pallas kernels: 0 us -> 144 us
  waiting for transfers between devices: 109 us -> 0 us
  local copies, waits for them, and re-layouts: 23.7 us -> 0.45 us
  other arithmetic: 18.3 us -> 2.18 us
  between operations: 14 us -> 0.03 us
    psum x1 -> x0, blocking collectives: 275 us -> none  [shards(): lax.psum(lax.dot_general(stacked, weighted, (((0,), (0,)), ((), ())), pre...]
    dot_general x3 -> x0, matrix products: 174 us -> none  [the longest x1 140 us: shards(): lax.dot_general(stacked, weighted, (((0,), (0,)), ((), ())), preferred_el...]
    pallas_call x0 -> x1, Pallas kernels: none -> 144 us  [shards(): pl.pallas_call(functools.partial(kernel, groups), out_shape=jax.ShapeDtyp...]
    all_gather x1 -> x0, waiting for transfers between devices: 60.1 us -> none  [shards(): arrived = lax.all_gather(rounded, ('site', 'col'), axis=0, tiled=True)]
    all_to_all x1 -> x0, waiting for transfers between devices: 48.8 us -> none  [shards(): slab = lax.all_to_all(panel, 'col', split_axis=1, concat_axis=2, tiled=True)]
    neg x3 -> x0, other arithmetic: 12.8 us -> none  [the longest x1 6.12 us: commute(): -py_imag]
    unnamed x13 -> x0, local copies, waits for them, and re-layouts: 12.1 us -> none
    all_to_all x1 -> x0, local copies, waits for them, and re-layouts: 6.5 us -> none  [shards(): slab = lax.all_to_all(panel, 'col', split_axis=1, concat_axis=2, tiled=True)]
  transfers between devices with their start and end apart: 2 -> 0, of which waited for: 2 -> 0; matrix products, arithmetic and copies ran while one was open for 0% -> 0% of each run, Pallas kernels for 0% -> 0%
where the time goes in v1:
time: 149 us; the launch traced here: 147 us
  Pallas kernels  144 us (97%)
  other arithmetic  2.18 us (1%)
    pallas_call x1, Pallas kernels, shards(): pl.pallas_call(functools.partial(kernel, groups), out_shape=jax.ShapeDtyp...  144 us

profile of v1, /device:TPU:0, one launch (start us, length us, event | category | flops | bytes accessed | tf_op | source)
XLA Modules:
  0.0 146.8 jit_solution(7332782522731983098)
XLA Ops:
  0.0 0.7 convert_add_fusion.1
  0.7 0.7 convert_add_fusion
  1.4 0.2 copy.5.cy_ref
  1.6 0.2 copy.4.cx_ref
  1.8 144.2 %shard_map.37 = f32[1024,1]{1,0:T(8,128)S(1)} custom-call(bf16[2,2048,512]{2,1,0:T(8,128)(2,1)} %panel_ref.1, f32[1024,1]{1,0:T(8,128)S(1)} %copy.4.cx_ref, f32[1024,1]{1,0:T(8,128)S(1)} %copy.5.cy_ref), custom_call_target="tpu_custom_call" | custom-call | tf_op jit(solution)/shard_map/pallas_call | solution.py:236
  146.0 0.8 reduce

commit v2 on v0

v2 whole, which is shorter than its diff:
```python
import functools
import math

import jax
import jax.numpy as jnp
from jax import lax
from jax.experimental import pallas as pl
from jax.experimental.pallas import tpu as pltpu
from jax.sharding import PartitionSpec as P

LX = 256
MESH = pl.DeviceIdType.MESH
TN = (((0,), (0,)), ((), ()))
BLOCK = 256
PIECES = 4
STEP = 64


def kernel(groups, panel_ref, centre_ref, out_ref, mine, got, theirs, weights,
           dacc, dstage0, drecv0, dstage1, drecv1, dstage2, drecv2, dfull,
           acc, stage0, recv0, stage1, recv1, stage2, recv2, stage3, recv3, ofull, turned, pq,
           local_sem, centre_sem, swap_send, swap_recv,
           dpair_send, dpair_recv, dgroup_send, dgroup_recv, dgather_send, dgather_recv,
           dspread_send, dspread_recv,
           pair_send, pair_recv, group_send, group_recv,
           gather_send, gather_recv, spread_send, spread_recv):
    rows, half = got.shape[1], got.shape[2]
    width, part_cols = 2 * half, half // 2
    site, col = lax.axis_index("site"), lax.axis_index("col")
    core = site % 2
    pair = (site // 2) % 2
    group = site // 4
    other_core = (site + 1 - 2 * core, col)
    other_pair = (site + 2 - 4 * pair, col)
    other_col = (site, 1 - col)

    def peer(step):
        return (((group + step) % groups) * 4 + pair * 2 + core, col)

    barrier = pltpu.get_barrier_semaphore()
    for target in [other_core, other_pair, other_col] + [peer(d) for d in range(1, groups)]:
        pl.semaphore_signal(barrier, inc=1, device_id=target, device_id_type=MESH)
    pl.semaphore_wait(barrier, 3 + groups - 1)

    def send(src, dst, send_sem, recv_sem, target):
        copy = pltpu.make_async_remote_copy(
            src_ref=src, dst_ref=dst, send_sem=send_sem, recv_sem=recv_sem,
            device_id=target, device_id_type=MESH)
        copy.start()
        return copy

    def aligned(start, size):
        return pl.ds(pl.multiple_of(start, 16), size)

    def wide(start, size):
        return pl.ds(pl.multiple_of(start, 256), size)

    tall = rows // PIECES
    centres = send(centre_ref, theirs, centre_sem.at[0], centre_sem.at[1], other_col)
    swaps = []
    for k in range(PIECES):
        swaps.append(send(panel_ref.at[:, wide((1 - col) * rows + k * tall, tall), :],
                          got.at[:, pl.ds(k * tall, tall), :],
                          swap_send.at[k], swap_recv.at[k], other_col))
    locals_ = []
    for n, at in enumerate((wide(col * rows, rows), wide((1 - col) * rows, rows))):
        copy = pltpu.make_async_copy(panel_ref.at[:, at, :], mine.at[:, at, :], local_sem.at[n])
        copy.start()
        locals_.append(copy)

    def spread_weights(n, source):
        for h in range(2):
            for i in range(rows // 128):
                line = jnp.broadcast_to(source[h, i:i + 1, :], (128, 128))
                weights[h, n, i * 128:(i + 1) * 128, :] = line.T

    def scaled(ref, h, n, weight_rows, at, lanes):
        line = weights[h, n, weight_rows, :]
        weight = jnp.concatenate([line] * (BLOCK // 128), axis=1)
        real = ref[0, at, lanes].astype(jnp.float32)
        imag = ref[1, at, lanes].astype(jnp.float32)
        return ((weight * (real + imag)).astype(jnp.bfloat16),
                (weight * (imag - real)).astype(jnp.bfloat16))

    def gram(first, second, ref, at):
        part = lax.dot_general(first, ref[0, at, :], TN, preferred_element_type=jnp.float32)
        return part + lax.dot_general(second, ref[1, at, :], TN, preferred_element_type=jnp.float32)

    def near_gram(n):
        start = (col if n == 0 else 1 - col) * rows

        @pl.loop(0, half // BLOCK)
        def _(j):
            lanes = wide(j * BLOCK, BLOCK)
            for h in range(2):
                total = None
                for k in range(2):
                    span = rows // 2
                    at = wide(start + k * span, span)
                    first, second = scaled(mine, h, n, pl.ds(k * span, span), at, lanes)
                    part = gram(first, second, mine, at)
                    total = part if total is None else total + part
                if n == 0:
                    dacc[h, lanes, :] = total
                else:
                    dacc[h, lanes, :] += total

    def far_gram(k, h):
        mine_at, got_at = wide(col * rows + k * tall, tall), pl.ds(k * tall, tall)

        @pl.loop(0, half // BLOCK)
        def _(j):
            lanes = wide(j * BLOCK, BLOCK)
            for left, left_at, right, right_at, base in (
                    (mine, mine_at, got, got_at, col * half),
                    (got, got_at, mine, mine_at, (1 - col) * half)):
                first, second = scaled(left, h, 0, got_at, left_at, lanes)
                part = gram(first, second, right, right_at)
                place = wide(base + j * BLOCK, BLOCK)
                if k == 0:
                    acc[h, place, :] = part
                else:
                    acc[h, place, :] += part

    own = pl.ds(pl.multiple_of(core * part_cols, part_cols), part_cols)
    away = pl.ds(pl.multiple_of((1 - core) * part_cols, part_cols), part_cols)
    quarter = half // 2
    chunk = quarter // groups

    def strips(count, body):
        @pl.loop(0, count // STEP)
        def _(i):
            body(i * STEP)

    def d0():
        def body(i):
            at = aligned(i, STEP)
            for h in range(2):
                dstage0[h, at, :] = dacc[h, at, away].astype(jnp.bfloat16)
        strips(half, body)
        return [send(dstage0, drecv0, dpair_send.at[0], dpair_recv.at[0], other_core)]

    def d1():
        def gone(i):
            at = aligned((1 - pair) * quarter + i, STEP)
            for h in range(2):
                dstage1[h, aligned(i, STEP), :] = (
                    dacc[h, at, own] + drecv0[h, at, :].astype(jnp.float32)).astype(jnp.bfloat16)

        def kept(i):
            at = aligned(pair * quarter + i, STEP)
            for h in range(2):
                dacc[h, at, own] += drecv0[h, at, :].astype(jnp.float32)
        strips(quarter, gone)
        copy = send(dstage1, drecv1, dpair_send.at[1], dpair_recv.at[1], other_pair)
        strips(quarter, kept)
        return [copy]

    def d2():
        def body(i):
            at, inner = aligned(pair * quarter + i, STEP), aligned(i, STEP)
            for h in range(2):
                total = dacc[h, at, own] + drecv1[h, inner, :].astype(jnp.float32)
                dacc[h, at, own] = total
                dstage2[h, inner, :] = total.astype(jnp.bfloat16)
        strips(quarter, body)
        copies = []
        for d in range(1, groups):
            to = (group + d) % groups
            copies.append(send(dstage2.at[:, aligned(to * chunk, chunk), :], drecv2.at[:, d - 1],
                               dgroup_send.at[d - 1], dgroup_recv.at[d - 1], peer(d)))
        return copies

    def dgather(n, which):
        place = dfull.at[:, aligned(which * half + pair * quarter + group * chunk, chunk), own]
        return [send(place, place, dgather_send.at[n, d - 1], dgather_recv.at[n, d - 1], peer(d))
                for d in range(1, groups)]

    def d3():
        at = aligned(pair * quarter + group * chunk, chunk)
        place = aligned(col * half + pair * quarter + group * chunk, chunk)
        for h in range(2):
            total = dacc[h, at, own]
            for d in range(1, groups):
                total += drecv2[h, d - 1].astype(jnp.float32)
            dfull[h, place, own] = total.astype(jnp.bfloat16)
        ref = dfull.at[:, place, own]
        return [send(ref, ref, dspread_send.at[0], dspread_recv.at[0], other_col)], dgather(0, col)

    def d5():
        copies = []
        for n, which in enumerate((col, 1 - col)):
            ref = dfull.at[:, wide(which * half + pair * quarter, quarter), own]
            copies.append(send(ref, ref, dspread_send.at[1 + n], dspread_recv.at[1 + n], other_pair))
        return copies

    def d6():
        ref = dfull.at[:, :, own]
        return [send(ref, ref, dspread_send.at[3], dspread_recv.at[3], other_core)]

    bits = [(col, pair), (pair, col)]
    targets = [(other_col, other_pair), (other_pair, other_col)]
    base1 = [bits[h][0] * half for h in range(2)]
    base2 = [base1[h] + bits[h][1] * quarter for h in range(2)]
    base3 = [base2[h] + group * chunk for h in range(2)]

    def o0(h):
        def body(i):
            at = aligned(i, STEP)
            stage0[h, at, :] = acc[h, at, away].astype(jnp.bfloat16)
        strips(width, body)
        return [send(stage0.at[h], recv0.at[h], pair_send.at[0, h], pair_recv.at[0, h], other_core)]

    def o1(h):
        def gone(i):
            at = aligned((1 - bits[h][0]) * half + i, STEP)
            stage1[h, aligned(i, STEP), :] = (
                acc[h, at, own] + recv0[h, at, :].astype(jnp.float32)).astype(jnp.bfloat16)

        def kept(i):
            at = aligned(base1[h] + i, STEP)
            acc[h, at, own] += recv0[h, at, :].astype(jnp.float32)
        strips(half, gone)
        copy = send(stage1.at[h], recv1.at[h], pair_send.at[1, h], pair_recv.at[1, h], targets[h][0])
        strips(half, kept)
        return [copy]

    def o2(h):
        def gone(i):
            inner = aligned((1 - bits[h][1]) * quarter + i, STEP)
            at = aligned(base1[h] + (1 - bits[h][1]) * quarter + i, STEP)
            stage2[h, aligned(i, STEP), :] = (
                acc[h, at, own] + recv1[h, inner, :].astype(jnp.float32)).astype(jnp.bfloat16)

        def kept(i):
            inner = aligned(bits[h][1] * quarter + i, STEP)
            at = aligned(base2[h] + i, STEP)
            acc[h, at, own] += recv1[h, inner, :].astype(jnp.float32)
        strips(quarter, gone)
        copy = send(stage2.at[h], recv2.at[h], pair_send.at[2, h], pair_recv.at[2, h], targets[h][1])
        strips(quarter, kept)
        return [copy]

    def o3(h):
        def body(i):
            inner, at = aligned(i, STEP), aligned(base2[h] + i, STEP)
            total = acc[h, at, own] + recv2[h, inner, :].astype(jnp.float32)
            acc[h, at, own] = total
            stage3[h, inner, :] = total.astype(jnp.bfloat16)
        strips(quarter, body)
        copies = []
        for d in range(1, groups):
            to = (group + d) % groups
            copies.append(send(stage3.at[h, aligned(to * chunk, chunk), :], recv3.at[h, d - 1],
                               group_send.at[h, d - 1], group_recv.at[h, d - 1], peer(d)))
        return copies

    def o4(h):
        at = aligned(base3[h], chunk)
        total = acc[h, at, own]
        for d in range(1, groups):
            total += recv3[h, d - 1].astype(jnp.float32)
        ofull[h, at, own] = total.astype(jnp.bfloat16)
        place = ofull.at[h, at, own]
        return [send(place, place, gather_send.at[h, d - 1], gather_recv.at[h, d - 1], peer(d))
                for d in range(1, groups)]

    def spread(h, at, which, target):
        place = ofull.at[h, at, own]
        return [send(place, place, spread_send.at[which, h], spread_recv.at[which, h], target)]

    def o5(h):
        return spread(h, wide(base2[h], quarter), 0, targets[h][1])

    def o6(h):
        return spread(h, wide(base1[h], half), 1, targets[h][0])

    def o7(h):
        return spread(h, pl.ds(0, width), 2, other_core)

    dot = functools.partial(jnp.dot, preferred_element_type=jnp.float32)
    deep = 256

    def project_near(side, j):
        which = col if side == 0 else 1 - col
        lanes = pl.ds(j * BLOCK, BLOCK)
        for h in range(2):
            turned[h] = dfull[h, wide(which * half + j * BLOCK, BLOCK), :].T

        @pl.loop(0, rows // deep)
        def _(r):
            here = wide(r * deep, deep)
            if side == 0:
                at = wide(col * rows + r * deep, deep)
                real, imag = mine[0, at, :], mine[1, at, :]
            else:
                real, imag = got[0, here, :], got[1, here, :]
            for h in range(2):
                straight = dfull[h, wide(which * half, half), lanes]
                pq[h, side, here, lanes] = dot(real, turned[h]) + dot(imag, straight)
                pq[2 + h, side, here, lanes] = dot(imag, turned[h]) - dot(real, straight)

    def project_far(side, j):
        which = col if side == 0 else 1 - col
        lanes = pl.ds(j * BLOCK, BLOCK)
        for h in range(2):
            turned[h] = ofull[h, wide(which * half + j * BLOCK, BLOCK), :].T

        @pl.loop(0, rows // deep)
        def _(r):
            here = wide(r * deep, deep)
            if side == 1:
                at = wide(col * rows + r * deep, deep)
                real, imag = mine[0, at, :], mine[1, at, :]
            else:
                real, imag = got[0, here, :], got[1, here, :]
            ps, qs = [], []
            for h in range(2):
                straight = ofull[h, wide((1 - which) * half, half), lanes]
                ps.append(pq[h, side, here, lanes] + dot(real, turned[h]) + dot(imag, straight))
                qs.append(pq[2 + h, side, here, lanes] + dot(imag, turned[h]) - dot(real, straight))
            term = 2.0 * math.pi * jnp.sum(qs[0] * ps[1] - ps[0] * qs[1], axis=1, keepdims=True)
            if side == 0 and j == 0:
                out_ref[here, :] = term
            else:
                out_ref[here, :] += term

    def finish(copies):
        for copy in copies:
            copy.wait()

    spread_weights(0, centre_ref)
    locals_[0].wait()
    near_gram(0)
    centres.wait()
    spread_weights(1, theirs)
    locals_[1].wait()
    near_gram(1)
    moving = d0()
    finish(moving)
    moving = d1()
    finish(moving)
    moving = d2()
    swaps[0].wait()
    far_gram(0, 0)
    far_gram(0, 1)
    finish(moving)
    across, around = d3()
    swaps[1].wait()
    far_gram(1, 0)
    far_gram(1, 1)
    finish(across)
    around2 = dgather(1, 1 - col)
    finish(around)
    swaps[2].wait()
    far_gram(2, 0)
    far_gram(2, 1)
    finish(around2)
    moving = d5()
    swaps[3].wait()
    flight = [None, None]
    for h in range(2):
        far_gram(3, h)
        flight[h] = o0(h)
    finish(moving)
    moving = d6()

    def advance(begin):
        for h in range(2):
            finish(flight[h])
            flight[h] = begin(h)

    advance(o1)
    finish(moving)
    project_near(0, 0)
    advance(o2)
    project_near(0, 1)
    advance(o3)
    advance(o4)
    advance(o5)
    project_near(1, 0)
    advance(o6)
    project_near(1, 1)
    advance(o7)
    for h in range(2):
        finish(flight[h])
    for side in range(2):
        for j in range(half // BLOCK):
            project_far(side, j)


def shards(panel, xs, ys):
    rows = panel.shape[1] // lax.axis_size("col")
    half = panel.shape[2]
    width = half * lax.axis_size("col")
    devices = lax.axis_size("site") * lax.axis_size("col")
    groups = lax.axis_size("site") // 4
    lat_y = rows * devices // LX
    centre_x = xs.astype(jnp.float32) - (LX - 1) / 2.0
    centre_y = ys.astype(jnp.float32) - (lat_y - 1) / 2.0
    centre = jnp.stack([centre_x, centre_y]).reshape(2, rows // 128, 128)
    quarter = half // 2
    chunk = quarter // groups
    dma = pltpu.SemaphoreType.DMA
    b16, f32 = jnp.bfloat16, jnp.float32
    vmem = pl.BlockSpec(memory_space=pltpu.VMEM)
    out = pl.pallas_call(
        functools.partial(kernel, groups),
        out_shape=jax.ShapeDtypeStruct((rows, 1), f32),
        in_specs=[pl.BlockSpec(memory_space=pl.ANY), vmem],
        out_specs=vmem,
        scratch_shapes=[
            pltpu.VMEM((2, 2 * rows, half), b16),
            pltpu.VMEM((2, rows, half), b16),
            pltpu.VMEM((2, rows // 128, 128), f32),
            pltpu.VMEM((2, 2, rows, 128), f32),
            pltpu.VMEM((2, half, half), f32),
            pltpu.VMEM((2, half, quarter), b16),
            pltpu.VMEM((2, half, quarter), b16),
            pltpu.VMEM((2, quarter, quarter), b16),
            pltpu.VMEM((2, quarter, quarter), b16),
            pltpu.VMEM((2, quarter, quarter), b16),
            pltpu.VMEM((2, groups - 1, chunk, quarter), b16),
            pltpu.VMEM((2, width, half), b16),
            pltpu.VMEM((2, width, half), f32),
            pltpu.VMEM((2, width, quarter), b16),
            pltpu.VMEM((2, width, quarter), b16),
            pltpu.VMEM((2, half, quarter), b16),
            pltpu.VMEM((2, half, quarter), b16),
            pltpu.VMEM((2, quarter, quarter), b16),
            pltpu.VMEM((2, quarter, quarter), b16),
            pltpu.VMEM((2, quarter, quarter), b16),
            pltpu.VMEM((2, groups - 1, chunk, quarter), b16),
            pltpu.VMEM((2, width, half), b16),
            pltpu.VMEM((2, half, BLOCK), b16),
            pltpu.VMEM((4, 2, rows, half), f32),
            dma((2,)), dma((2,)), dma((PIECES,)), dma((PIECES,)),
            dma((2,)), dma((2,)), dma((groups - 1,)), dma((groups - 1,)),
            dma((2, groups - 1)), dma((2, groups - 1)), dma((4,)), dma((4,)),
            dma((3, 2)), dma((3, 2)), dma((2, groups - 1)), dma((2, groups - 1)),
            dma((2, groups - 1)), dma((2, groups - 1)), dma((3, 2)), dma((3, 2)),
        ],
        compiler_params=pltpu.CompilerParams(
            collective_id=0, has_side_effects=True, vmem_limit_bytes=56 * 1024 * 1024),
    )(panel, centre)
    return out[:, 0]


def solution(mesh):
    placed = (P(None, "site", "col"), P(("site", "col")), P(("site", "col")))
    return jax.shard_map(
        shards, mesh=mesh, in_specs=placed, out_specs=P(("site", "col")), check_vma=False
    )
```

time: 627 us -> 127 us (0.20); the launches traced: 620 us -> 126 us
  blocking collectives: 275 us -> 0 us
  matrix products: 174 us -> 0 us
  Pallas kernels: 0 us -> 123 us
  waiting for transfers between devices: 109 us -> 0 us
  local copies, waits for them, and re-layouts: 23.7 us -> 0 us
  other arithmetic: 18.3 us -> 3.15 us
  between operations: 14 us -> 0.01 us
    psum x1 -> x0, blocking collectives: 275 us -> none  [shards(): lax.psum(lax.dot_general(stacked, weighted, (((0,), (0,)), ((), ())), pre...]
    dot_general x3 -> x0, matrix products: 174 us -> none  [the longest x1 140 us: shards(): lax.dot_general(stacked, weighted, (((0,), (0,)), ((), ())), preferred_el...]
    pallas_call x0 -> x1, Pallas kernels: none -> 123 us  [shards(): pl.pallas_call(functools.partial(kernel, groups), out_shape=jax.ShapeDtyp...]
    all_gather x1 -> x0, waiting for transfers between devices: 60.1 us -> none  [shards(): arrived = lax.all_gather(rounded, ('site', 'col'), axis=0, tiled=True)]
    all_to_all x1 -> x0, waiting for transfers between devices: 48.8 us -> none  [shards(): slab = lax.all_to_all(panel, 'col', split_axis=1, concat_axis=2, tiled=True)]
    neg x3 -> x0, other arithmetic: 12.8 us -> none  [the longest x1 6.12 us: commute(): -py_imag]
    unnamed x13 -> x0, local copies, waits for them, and re-layouts: 12.1 us -> none
    all_to_all x1 -> x0, local copies, waits for them, and re-layouts: 6.5 us -> none  [shards(): slab = lax.all_to_all(panel, 'col', split_axis=1, concat_axis=2, tiled=True)]
  transfers between devices with their start and end apart: 2 -> 0, of which waited for: 2 -> 0; matrix products, arithmetic and copies ran while one was open for 0% -> 0% of each run, Pallas kernels for 0% -> 0%
where the time goes in v2:
time: 127 us; the launch traced here: 126 us
  Pallas kernels  123 us (97%)
  other arithmetic  3.15 us (2%)
    pallas_call x1, Pallas kernels, shards(): pl.pallas_call(functools.partial(kernel, groups), out_shape=jax.ShapeDtyp...  123 us

profile of v2, /device:TPU:0, one launch (start us, length us, event | category | flops | bytes accessed | tf_op | source)
XLA Modules:
  0.0 126.4 jit_solution(10519194373620649223)
XLA Ops:
  0.0 0.7 add_bitcast_fusion
  0.7 0.6 pad_maximum_fusion.centre_ref
  1.3 123.3 %shard_map.37 = f32[1024,1]{1,0:T(8,128)} custom-call(bf16[2,2048,512]{2,1,0:T(8,128)(2,1)} %panel_ref.1, f32[2,8,128]{2,1,0:T(8,128)} %pad_maximum_fusion.centre_ref), custom_call_target="tpu_custom_call" | custom-call | tf_op jit(solution)/shard_map/pallas_call | solution.py:407
  124.6 1.8 %reduce = f32[1024]{0:T(1024)} reduce(f32[1024,1]{1,0:T(8,128)} %shard_map.37, f32[]{:T(128)} %constant.6), dimensions={1}, to_apply=%pallas_call.3.reduce_sub_computation | reduce | bytes 8196 | tf_op jit(solution)/shard_map/pallas_call | solution.py:407

commit v3 on v2

--- a/solution.py
+++ b/solution.py
@@ -57,11 +57,13 @@
 
     tall = rows // PIECES
     centres = send(centre_ref, theirs, centre_sem.at[0], centre_sem.at[1], other_col)
-    swaps = []
-    for k in range(PIECES):
-        swaps.append(send(panel_ref.at[:, wide((1 - col) * rows + k * tall, tall), :],
-                          got.at[:, pl.ds(k * tall, tall), :],
-                          swap_send.at[k], swap_recv.at[k], other_col))
+
+    def swap(k):
+        return send(panel_ref.at[:, wide((1 - col) * rows + k * tall, tall), :],
+                    got.at[:, pl.ds(k * tall, tall), :],
+                    swap_send.at[k], swap_recv.at[k], other_col)
+
+    swaps = [swap(0), swap(1)]
     locals_ = []
     for n, at in enumerate((wide(col * rows, rows), wide((1 - col) * rows, rows))):
         copy = pltpu.make_async_copy(panel_ref.at[:, at, :], mine.at[:, at, :], local_sem.at[n])
@@ -341,11 +343,13 @@
     moving = d1()
     finish(moving)
     moving = d2()
+    swaps.append(swap(2))
     swaps[0].wait()
     far_gram(0, 0)
     far_gram(0, 1)
     finish(moving)
     across, around = d3()
+    swaps.append(swap(3))
     swaps[1].wait()
     far_gram(1, 0)
     far_gram(1, 1)
@@ -362,8 +366,6 @@
     for h in range(2):
         far_gram(3, h)
         flight[h] = o0(h)
-    finish(moving)
-    moving = d6()
 
     def advance(begin):
         for h in range(2):
@@ -372,11 +374,13 @@
 
     advance(o1)
     finish(moving)
+    moving = d6()
+    advance(o2)
+    advance(o3)
+    finish(moving)
     project_near(0, 0)
-    advance(o2)
+    advance(o4)
     project_near(0, 1)
-    advance(o3)
-    advance(o4)
     advance(o5)
     project_near(1, 0)
     advance(o6)

time: 127 us -> 114 us (0.90)
  Pallas kernels: 123 us -> 111 us
    pallas_call x1, Pallas kernels: 123 us -> 111 us  [shards(): pl.pallas_call(functools.partial(kernel, groups), out_shape=jax.ShapeDtyp...]
where the time goes in v3:
time: 114 us
  Pallas kernels  111 us (97%)
  other arithmetic  3.15 us (3%)
    pallas_call x1, Pallas kernels, shards(): pl.pallas_call(functools.partial(kernel, groups), out_shape=jax.ShapeDtyp...  111 us

profile of v3, /device:TPU:0, one launch (start us, length us, event | category | flops | bytes accessed | tf_op | source)
XLA Modules:
  0.0 113.8 jit_solution(13868363022321639844)
XLA Ops:
  0.0 0.7 add_bitcast_fusion
  0.7 0.6 pad_maximum_fusion.centre_ref
  1.3 110.6 %shard_map.37 = f32[1024,1]{1,0:T(8,128)} custom-call(bf16[2,2048,512]{2,1,0:T(8,128)(2,1)} %panel_ref.1, f32[2,8,128]{2,1,0:T(8,128)} %pad_maximum_fusion.centre_ref), custom_call_target="tpu_custom_call" | custom-call | tf_op jit(solution)/shard_map/pallas_call | solution.py:411
  112.0 1.8 %reduce = f32[1024]{0:T(1024)} reduce(f32[1024,1]{1,0:T(8,128)} %shard_map.37, f32[]{:T(128)} %constant.6), dimensions={1}, to_apply=%pallas_call.3.reduce_sub_computation | reduce | bytes 8196 | tf_op jit(solution)/shard_map/pallas_call | solution.py:411

commit v4 on v3

--- a/solution.py
+++ b/solution.py
@@ -12,6 +12,7 @@
 MESH = pl.DeviceIdType.MESH
 TN = (((0,), (0,)), ((), ()))
 BLOCK = 256
+GRAM = 512
 PIECES = 4
 STEP = 64
 
@@ -78,7 +79,7 @@
 
     def scaled(ref, h, n, weight_rows, at, lanes):
         line = weights[h, n, weight_rows, :]
-        weight = jnp.concatenate([line] * (BLOCK // 128), axis=1)
+        weight = jnp.concatenate([line] * (GRAM // 128), axis=1)
         real = ref[0, at, lanes].astype(jnp.float32)
         imag = ref[1, at, lanes].astype(jnp.float32)
         return ((weight * (real + imag)).astype(jnp.bfloat16),
@@ -91,9 +92,9 @@
     def near_gram(n):
         start = (col if n == 0 else 1 - col) * rows
 
-        @pl.loop(0, half // BLOCK)
+        @pl.loop(0, half // GRAM)
         def _(j):
-            lanes = wide(j * BLOCK, BLOCK)
+            lanes = wide(j * GRAM, GRAM)
             for h in range(2):
                 total = None
                 for k in range(2):
@@ -110,15 +111,15 @@
     def far_gram(k, h):
         mine_at, got_at = wide(col * rows + k * tall, tall), pl.ds(k * tall, tall)
 
-        @pl.loop(0, half // BLOCK)
+        @pl.loop(0, half // GRAM)
         def _(j):
-            lanes = wide(j * BLOCK, BLOCK)
+            lanes = wide(j * GRAM, GRAM)
             for left, left_at, right, right_at, base in (
                     (mine, mine_at, got, got_at, col * half),
                     (got, got_at, mine, mine_at, (1 - col) * half)):
                 first, second = scaled(left, h, 0, got_at, left_at, lanes)
                 part = gram(first, second, right, right_at)
-                place = wide(base + j * BLOCK, BLOCK)
+                place = wide(base + j * GRAM, GRAM)
                 if k == 0:
                     acc[h, place, :] = part
                 else:
@@ -281,7 +282,7 @@
         return spread(h, pl.ds(0, width), 2, other_core)
 
     dot = functools.partial(jnp.dot, preferred_element_type=jnp.float32)
-    deep = 256
+    deep = 512
 
     def project_near(side, j):
         which = col if side == 0 else 1 - col

time: 114 us -> 112 us (0.982)
  Pallas kernels: 111 us -> 108 us
    pallas_call x1, Pallas kernels: 111 us -> 108 us  [shards(): pl.pallas_call(functools.partial(kernel, groups), out_shape=jax.ShapeDtyp...]
where the time goes in v4:
time: 112 us
  Pallas kernels  108 us (96%)
  other arithmetic  3.15 us (3%)
    pallas_call x1, Pallas kernels, shards(): pl.pallas_call(functools.partial(kernel, groups), out_shape=jax.ShapeDtyp...  108 us

profile of v4, /device:TPU:0, one launch (start us, length us, event | category | flops | bytes accessed | tf_op | source)
XLA Modules:
  0.0 111.6 jit_solution(17260184505173925275)
XLA Ops:
  0.0 0.7 add_bitcast_fusion
  0.7 0.6 pad_maximum_fusion.centre_ref
  1.3 108.5 %shard_map.37 = f32[1024,1]{1,0:T(8,128)} custom-call(bf16[2,2048,512]{2,1,0:T(8,128)(2,1)} %panel_ref.1, f32[2,8,128]{2,1,0:T(8,128)} %pad_maximum_fusion.centre_ref), custom_call_target="tpu_custom_call" | custom-call | tf_op jit(solution)/shard_map/pallas_call | solution.py:412
  109.8 1.8 %reduce = f32[1024]{0:T(1024)} reduce(f32[1024,1]{1,0:T(8,128)} %shard_map.37, f32[]{:T(128)} %constant.6), dimensions={1}, to_apply=%pallas_call.3.reduce_sub_computation | reduce | bytes 8196 | tf_op jit(solution)/shard_map/pallas_call | solution.py:412
